TPU v7x, 32 devices: a whole 2x2x4 slice. The times are simulated.
32 devices in a mesh: parts: 2 (over y), hold: 16 (over z, x, core).
Axes of the slice: x: 2, y: 2, z: 4, core: 2. Of those that a mesh axis runs over, the one named last changes fastest.
Arguments:
- embeddings: float32 [16384, 768], P(('parts', 'hold')), parts along dimension 0
- cluster_id: int32 [16384], P(('parts', 'hold')), parts along dimension 0, may hold values from 0 to 127, as said below
- cluster_rank: int32 [16384], P(('parts', 'hold')), parts along dimension 0, may hold values from 0 to 767, as said below
Outputs:
- maxima: float32 [16384], P(('parts', 'hold')), parts along dimension 0
There are 2 independent parts, one for each index of `parts`. A program takes and returns all parts, laid end to end along the dimension named above; each array names one. Nothing has to cross between parts.
Inputs may be any that keep to these rules, and one draw needn't show every extreme that they name: `cluster_id`: clusters 8 * j to 8 * j + 7 form owner block j. The rows of one device fall into any one owner block at most 48 times; in every draw one owner block gets exactly 48 rows from every device. `cluster_rank`: within each cluster the ranks of its rows are 0 to its size - 1, each once. No cluster has more than 16 * 48 rows; in every draw one cluster has exactly that many.
All inputs are finite; a program needn't handle non-finite values.
Results may differ from a plain program's by a relative error of at most 0.0003.
Values may be sent and summed in bfloat16 or wider, within the bound.
A program may use at most 64 MiB of HBM per device.

v0:
```python
import math

import jax
import jax.numpy as jnp
from jax import lax
from jax.sharding import PartitionSpec as P

CL_DEV = 8


epsilon = 1e-06
floor_value = -1.0


def unit_rows(embeddings):
    squares = jnp.sum(embeddings * embeddings, axis=1, keepdims=True)
    return (embeddings * lax.rsqrt(squares + epsilon)).astype(jnp.bfloat16)


def product(left_rows, right_rows):
    return lax.dot_general(
        left_rows, right_rows, (((1,), (1,)), ((), ())), preferred_element_type=jnp.float32
    )


def masked_best(scores, query_labels, query_orders, key_labels, key_orders):
    allowed = (key_labels[None, :] == query_labels[:, None]) & (
        key_orders[None, :] < query_orders[:, None]
    )
    return jnp.max(jnp.where(allowed, scores, floor_value), axis=1)


def block_size(total_rows):
    return math.gcd(total_rows, 512)


def block_starts(total_rows, block_rows):
    return jnp.arange(total_rows // block_rows, dtype=jnp.int32) * block_rows


def take_block(source_array, offset, block_rows):
    return lax.dynamic_slice_in_dim(source_array, offset, block_rows, 0)


def dense_best(pieces, labels, orders):
    total_rows = labels.shape[0]
    block_rows = block_size(total_rows)

    def score_block(offset):
        scores = None
        for feature_piece in pieces:
            piece_term = product(take_block(feature_piece, offset, block_rows), feature_piece)
            scores = piece_term
        return masked_best(
            scores,
            take_block(labels, offset, block_rows),
            take_block(orders, offset, block_rows),
            labels,
            orders,
        )

    return lax.map(score_block, block_starts(total_rows, block_rows)).reshape(total_rows)


def shards(embeddings, cluster_id, cluster_rank):
    holders = lax.axis_size("hold")
    own_rows = embeddings.shape[0]
    features = embeddings.shape[1]
    slot_count = 3 * own_rows // (2 * holders)
    normed = unit_rows(embeddings)
    owners = cluster_id // CL_DEV
    member = (owners[:, None] == jnp.arange(holders, dtype=jnp.int32)[None, :]).astype(jnp.int32)
    earlier = jnp.cumsum(member, axis=0) - member
    target = owners * slot_count + jnp.sum(earlier * member, axis=1)
    outgoing = jnp.zeros((holders * slot_count, features), jnp.bfloat16).at[target].set(normed)
    labels_out = (
        jnp.full((holders * slot_count, 2), -1, jnp.int32)
        .at[target]
        .set(jnp.stack([cluster_id, cluster_rank], axis=1))
    )
    incoming, labels_in = (
        lax.all_to_all(outgoing, "hold", split_axis=0, concat_axis=0, tiled=True),
        lax.all_to_all(labels_out, "hold", split_axis=0, concat_axis=0, tiled=True),
    )
    labels = labels_in[:, 0]
    orders = labels_in[:, 1]
    maxima = dense_best((incoming,), labels, orders)
    returned = lax.all_to_all(maxima, "hold", split_axis=0, concat_axis=0, tiled=True)
    return returned[target]


def solution(mesh):
    in_specs = (P(("parts", "hold"), None), P(("parts", "hold")), P(("parts", "hold")))
    out_specs = P(("parts", "hold"))
    return jax.shard_map(shards, mesh=mesh, in_specs=in_specs, out_specs=out_specs, check_vma=False)
```

profile of v0, /device:TPU:0, one launch (start us, length us, event | category | flops | bytes accessed | tf_op | source)
XLA Modules:
  0.0 80.9 jit_solution(8727573491286402097)
XLA Ops:
  0.0 0.7 fusion.15
  0.7 0.7 add_select_fusion
  1.4 1.2 %reduce-window.6 = s32[16,4,128]{2,0,1:T(8,128)S(1)} reduce-window(s32[16,4,128]{2,0,1:T(8,128)S(1)} %fusion.11, s32[]{:T(128)} %constant.15.clone.1), window={size=1x1x128 pad=0_0x0_0x127_0}, to_apply=%region_0.0 | reduce-window | flops 1040384 | bytes 65540 | tf_op jit(solution)/shard_map/reduce-window
  2.5 0.2 slice_reduce_fusion
  2.8 0.1 fusion.10
  2.9 0.7 compare_select_fusion
  3.6 0.7 pad_add_fusion
  4.3 0.1 copy.13
  4.5 0.0 copy-start
  4.5 1.8 %scatter_custom_fusion = s32[768,2]{1,0:T(8,128)S(1)} fusion(s32[512]{0:T(512)S(1)} %compare_select_fusion, s32[512,2]{1,0:T(8,128)S(1)} %copy.13, s32[]{:T(128)} %constant.46.clone.1), kind=kCustom, calls=%fused_computation.12 | custom fusion | bytes 6148 | tf_op jit(solution)/shard_map/scatter | solution.py:79
  6.3 0.8 copy.14
  7.1 7.4 %all-to-all-start = ((s32[16,48,2]{1,2,0:T(2,128)}), s32[16,48,2]{1,2,0:T(2,128)S(1)}, u32[]{:S(2)}, u32[]{:S(2)}) async-start(s32[16,48,2]{1,2,0:T(2,128)} %copy.14), calls=%async_computation | async-start | bytes 32768 | tf_op jit(solution)/shard_map/all_to_all | solution.py:83
  14.4 1.6 %multiply_reduce_fusion = f32[512]{0:T(512)S(1)} fusion(f32[512,768]{1,0:T(8,128)} %param.5), kind=kLoop, calls=%fused_computation.8 | loop fusion | flops 785920 | bytes 1574912 | tf_op jit(solution)/shard_map/reduce_sum | solution.py:16
  16.0 0.0 copy-done
  16.0 3.6 %scatter_custom_fusion.1 = bf16[768,768]{1,0:T(8,128)(2,1)} fusion(s32[512]{0:T(512)S(1)} %compare_select_fusion, f32[512,768]{1,0:T(8,128)S(1)} %copy-done, f32[512]{0:T(512)S(1)} %add_rsqrt_fusion, bf16[]{:T(256)} %constant.42.clone.1), kind=kCustom, calls=%fused_computation.9 | custom fusion | flops 786432 | bytes 2754562 | tf_op jit(solution)/shard_map/scatter | solution.py:75
  19.7 1.3 %all-to-all-done = s32[16,48,2]{1,2,0:T(2,128)S(1)} async-done(((s32[16,48,2]{1,2,0:T(2,128)}), s32[16,48,2]{1,2,0:T(2,128)S(1)}, u32[]{:S(2)}, u32[]{:S(2)}) %all-to-all-start) | async-done | bytes 6176 | tf_op jit(solution)/shard_map/all_to_all | solution.py:83
  20.9 4.8 %all-to-all-start.1 = ((bf16[16,48,768]{2,1,0:T(8,128)(2,1)}), bf16[16,48,768]{2,1,0:T(8,128)(2,1)S(1)}, u32[]{:S(2)}, u32[]{:S(2)}) async-start(bf16[16,48,768]{2,1,0:T(8,128)(2,1)} %bitcast.7), calls=%async_computation.1 | async-start | bytes 2359296 | tf_op jit(solution)/shard_map/all_to_all | solution.py:82
  25.7 0.1 all_to_all.26
  25.8 25.0 %all-to-all-done.1 = bf16[16,48,768]{2,1,0:T(8,128)(2,1)S(1)} async-done(((bf16[16,48,768]{2,1,0:T(8,128)(2,1)}), bf16[16,48,768]{2,1,0:T(8,128)(2,1)S(1)}, u32[]{:S(2)}, u32[]{:S(2)}) %all-to-all-start.1) | async-done | bytes 1179680 | tf_op jit(solution)/shard_map/all_to_all | solution.py:82
  50.8 10.8 %while.10 = (s32[]{:T(128)}, f32[3,256]{1,0:T(4,128)S(1)}, s32[768,1]{0,1:T(1,128)S(1)}, s32[3]{0:T(128)S(1)}, s32[768]{0:T(1024)S(1)}, /*index=5*/s32[768,1]{0,...) while((s32[]{:T(128)}, f32[3,256]{1,0:T(4,128)S(1)}, ...), condition=%wide.region_8.9_spmd, body=%wide.region_6.8_spmd.sunk | while | flops 302972672 | bytes 1602739 | solution.py:62
  50.8 0.7 dynamic_slice.20
  53.6 0.1 dynamic_slice.21
  53.6 0.1 dynamic_slice.22
  53.7 0.6 fusion.21
  54.4 0.7 dynamic_slice.20
  57.2 0.1 dynamic_slice.21
  57.2 0.1 dynamic_slice.22
  57.3 0.6 fusion.21
  58.0 0.7 dynamic_slice.20
  60.8 0.1 dynamic_slice.21
  60.8 0.1 dynamic_slice.22
  60.9 0.6 fusion.21
  61.6 0.7 all_to_all.30
  62.3 7.5 %all-to-all-start.2 = ((f32[16,48,1]{1,2,0:T(1,128)}), f32[16,48,1]{1,2,0:T(1,128)S(1)}, u32[]{:S(2)}, u32[]{:S(2)}) async-start(f32[16,48,1]{1,2,0:T(1,128)} %all_to_all.30), calls=%async_computation.2 | async-start | bytes 16384 | tf_op jit(solution)/shard_map/all_to_all | solution.py:88
  69.8 6.4 %all-to-all-done.2 = f32[16,48,1]{1,2,0:T(1,128)S(1)} async-done(((f32[16,48,1]{1,2,0:T(1,128)}), f32[16,48,1]{1,2,0:T(1,128)S(1)}, u32[]{:S(2)}, u32[]{:S(2)}) %all-to-all-start.2) | async-done | bytes 3104 | tf_op jit(solution)/shard_map/all_to_all | solution.py:88
  76.2 0.5 broadcast.59
  76.7 0.7 reduce.11
  77.4 0.1 all_to_all.32
  77.5 3.4 %gather_fusion = f32[512]{0:T(512)} fusion(f32[768]{0:T(1024)S(1)} %all_to_all.32, s32[1024]{0:T(1024)S(1)} %pad_clamp_fusion), kind=kCustom, calls=%fused_computation | custom fusion | bytes 6144 | tf_op jit(solution)/shard_map/gather | solution.py:89
  (18 shorter events, 0.3 us)
Async XLA Ops:
  4.5 11.6 %copy-start = (f32[512,768]{1,0:T(8,128)S(1)}, f32[512,768]{1,0:T(8,128)}, u32[]{:S(2)}) copy-start(f32[512,768]{1,0:T(8,128)} %param.5) | copy-start | bytes 4718596
  7.1 13.9 %all-to-all-start = ((s32[16,48,2]{1,2,0:T(2,128)}), s32[16,48,2]{1,2,0:T(2,128)S(1)}, u32[]{:S(2)}, u32[]{:S(2)}) async-start(s32[16,48,2]{1,2,0:T(2,128)} %copy.14), calls=%async_computation | async-start | bytes 32768 | tf_op jit(solution)/shard_map/all_to_all | solution.py:83
  20.9 29.9 %all-to-all-start.1 = ((bf16[16,48,768]{2,1,0:T(8,128)(2,1)}), bf16[16,48,768]{2,1,0:T(8,128)(2,1)S(1)}, u32[]{:S(2)}, u32[]{:S(2)}) async-start(bf16[16,48,768]{2,1,0:T(8,128)(2,1)} %bitcast.7), calls=%async_computation.1 | async-start | bytes 2359296 | tf_op jit(solution)/shard_map/all_to_all | solution.py:82
  62.3 13.9 %all-to-all-start.2 = ((f32[16,48,1]{1,2,0:T(1,128)}), f32[16,48,1]{1,2,0:T(1,128)S(1)}, u32[]{:S(2)}, u32[]{:S(2)}) async-start(f32[16,48,1]{1,2,0:T(1,128)} %all_to_all.30), calls=%async_computation.2 | async-start | bytes 16384 | tf_op jit(solution)/shard_map/all_to_all | solution.py:88
where the time goes:
time: 81.4 us; the launch traced here: 80.9 us
  waiting for transfers between devices  32.6 us (40%)
  starting transfers between devices  19.6 us (24%)
  local copies, waits for them, and re-layouts  10.3 us (13%)
  other arithmetic  10.1 us (12%)
  loops' own time  6.28 us (8%)
  matrix products  1.84 us (2%)
    all_to_all x1, waiting for transfers between devices, shards(): lax.all_to_all(outgoing, 'hold', split_axis=0, concat_axis=0, tiled=True)  25 us
    all_to_all x1, starting transfers between devices, shards(): lax.all_to_all(maxima, 'hold', split_axis=0, concat_axis=0, tiled=True)  7.49 us
    all_to_all x1, starting transfers between devices, shards(): lax.all_to_all(labels_out, 'hold', split_axis=0, concat_axis=0, tiled=True)  7.36 us
    all_to_all x1, waiting for transfers between devices, shards(): lax.all_to_all(maxima, 'hold', split_axis=0, concat_axis=0, tiled=True)  6.39 us
    another operation x1, loops' own time, dense_best(): lax.map(score_block, block_starts(total_rows, block_rows))  6.28 us
    all_to_all x1, starting transfers between devices, shards(): lax.all_to_all(outgoing, 'hold', split_axis=0, concat_axis=0, tiled=True)  4.76 us
    scatter x1, other arithmetic, shards(): jnp.zeros((holders * slot_count, features), jnp.bfloat16).at[target]  3.64 us
    gather x1, local copies, waits for them, and re-layouts, shards(): return returned[target]  3.41 us
  transfers between devices with their start and end apart: 3, of which 3 were waited for; matrix products, arithmetic and copies ran while one was open for 7% of the time, Pallas kernels for 0%

commit v1 on v0

v1 whole, which is shorter than its diff:
```python
import functools

import jax
import jax.numpy as jnp
from jax import lax
from jax.experimental import pallas as pl
from jax.experimental.pallas import tpu as pltpu
from jax.sharding import PartitionSpec as P

CL_DEV = 8
GROUPS = 4
HALF = GROUPS // 2
RANKS = 1024
LANES = 128
QUERY_TILE = 256

epsilon = 1e-06
floor_value = -1.0
MESH = pl.DeviceIdType.MESH
f32, bf16, i32 = jnp.float32, jnp.bfloat16, jnp.int32


def group_towards(group, half, shift):
    return lax.rem(group // HALF + half, 2) * HALF + lax.rem(group % HALF + shift, HALF)


def group_from(group, half, shift):
    return lax.rem(group // HALF + half, 2) * HALF + lax.rem(group % HALF + HALF - shift, HALF)


def group_place(source, target):
    half = (source // HALF + target // HALF) % 2
    shift = (target % HALF - source % HALF + HALF) % HALF
    return half * HALF + shift


def pieces_of(values):
    first = values.astype(bf16)
    left = values - first.astype(f32)
    second = left.astype(bf16)
    third = (left - second.astype(f32)).astype(bf16)
    return jnp.concatenate([first.astype(f32), second.astype(f32), third.astype(f32)], axis=0).astype(bf16)


def dot(left, right, contract):
    return lax.dot_general(left, right, (contract, ((), ())), preferred_element_type=f32)


def kernel(
    holders, pad,
    emb_hbm, cid_ref, rank_ref, out_ref,
    emb, outgoing, incoming, lab_out, lab_in, bias, best, ret, back,
    emb_sem, self_sem, lab_send, lab_recv, row_send, row_recv, ret_send, ret_recv,
):
    size = holders // GROUPS
    rows, features = emb.shape
    group_rows = size * pad
    total = holders * pad
    me = lax.axis_index("hold")
    my_group, my_spot = me // size, me % size

    fetch = pltpu.make_async_copy(emb_hbm, emb, emb_sem)
    fetch.start()

    barrier = pltpu.get_barrier_semaphore()

    def greet(step, carry):
        pl.semaphore_signal(
            barrier, inc=1, device_id={"hold": lax.rem(me + step, holders)}, device_id_type=MESH
        )
        return carry

    lax.fori_loop(1, holders, greet, 0)

    def place_of(source, target):
        return group_place(source // size, target // size) * size + source % size

    def spots(half, shift):
        return (1, size) if half == 0 and shift == 0 else (0, size)

    def target_of(half, shift, i):
        return group_towards(my_group, half, shift) * size + lax.rem(my_spot + i, size)

    def source_of(half, shift, i):
        return group_from(my_group, half, shift) * size + lax.rem(my_spot + i, size)

    kinds = [(1, 0), (1, 1), (0, 1), (0, 0)]

    def over(half, shift, body):
        start, end = spots(half, shift)

        def step(i, carry):
            body(i)
            return carry

        lax.fori_loop(start, end, step, 0, unroll=True if size <= 4 else 1)

    cid = cid_ref[...]
    owner = cid // CL_DEV
    code = (cid - owner * CL_DEV + 1) * RANKS + rank_ref[...]
    ids = lax.broadcasted_iota(i32, (holders, rows), 0)
    member = owner == ids
    member16 = jnp.where(member, 1.0, 0.0).astype(bf16)
    before = jnp.where(
        lax.broadcasted_iota(i32, (rows, rows), 0) < lax.broadcasted_iota(i32, (rows, rows), 1), 1.0, 0.0
    ).astype(bf16)
    earlier = dot(member16, before, ((1,), (0,)))
    nth = jnp.sum(jnp.where(member, earlier, 0.0), axis=0, keepdims=True).astype(i32)
    target = owner * pad + nth

    spread = jnp.where(lax.broadcasted_iota(i32, (LANES, rows), 0) == nth, 1.0, 0.0).astype(bf16)
    high = (code // 128).astype(f32)
    low = (code % 128).astype(f32)
    parts = jnp.concatenate(
        [jnp.where(member, high, 0.0), jnp.where(member, low, 0.0)], axis=0
    ).astype(bf16)
    packed = dot(parts, spread, ((1,), (1,)))
    labels = (packed[:holders] * 128.0 + packed[holders:]).astype(i32)
    for j in range(holders):
        lab_out[j] = labels[j : j + 1]

    pl.semaphore_wait(barrier, holders - 1)

    def label_copy(half, shift, i):
        dest = target_of(half, shift, i)
        place = place_of(me, dest)
        return pltpu.make_async_remote_copy(
            src_ref=lab_out.at[dest], dst_ref=lab_in.at[place],
            send_sem=lab_send.at[dest], recv_sem=lab_recv.at[place],
            device_id={"hold": dest}, device_id_type=MESH,
        )

    for half, shift in kinds:
        over(half, shift, lambda i: label_copy(half, shift, i).start())
    own_label = pltpu.make_async_copy(lab_out.at[me], lab_in.at[place_of(me, me)], self_sem.at[0])
    own_label.start()

    fetch.wait()
    x = emb[...]
    squares = jnp.sum(x * x, axis=1, keepdims=True)
    normed = (x * lax.rsqrt(squares + epsilon)).astype(bf16)

    def row_copy(number, half, shift, i):
        dest = target_of(half, shift, i)
        place = place_of(me, dest)
        return pltpu.make_async_remote_copy(
            src_ref=outgoing.at[number * size + dest % size], dst_ref=incoming.at[place],
            send_sem=row_send.at[dest], recv_sem=row_recv.at[place],
            device_id={"hold": dest}, device_id_type=MESH,
        )

    slot_ids = lax.broadcasted_iota(i32, (group_rows, rows), 0)
    for number, (half, shift) in enumerate(kinds):
        base = group_towards(my_group, half, shift) * group_rows
        chosen = jnp.where(slot_ids == target - base, 1.0, 0.0).astype(bf16)
        laid = dot(chosen, normed, ((1,), (0,))).astype(bf16)
        outgoing[number * size : (number + 1) * size] = laid.reshape(size, pad, features)
        over(half, shift, lambda i: row_copy(number, half, shift, i).start())
    own_rows = pltpu.make_async_copy(
        outgoing.at[(GROUPS - 1) * size + my_spot], incoming.at[place_of(me, me)], self_sem.at[1]
    )
    own_rows.start()

    windows = total // LANES - 2

    def window_of(place):
        return jnp.minimum(place * pad // LANES, windows)

    places = place_of(me, ids)
    starts = places * pad - window_of(places) * LANES
    lane = jnp.sum(jnp.where(member, starts, 0), axis=0, keepdims=True) + nth
    pick = jnp.where(lax.broadcasted_iota(i32, (2 * LANES, rows), 0) == lane, 1.0, 0.0).astype(bf16)

    for half, shift in kinds:
        over(half, shift, lambda i: label_copy(half, shift, i).wait_send())
    own_label.wait()

    def wait_labels(half, shift, i):
        place = place_of(source_of(half, shift, i), me)
        pltpu.make_async_remote_copy(
            src_ref=lab_out.at[me], dst_ref=lab_in.at[place],
            send_sem=lab_send.at[me], recv_sem=lab_recv.at[place],
            device_id={"hold": me}, device_id_type=MESH,
        ).wait_recv()

    for half, shift in kinds:
        over(half, shift, lambda i: wait_labels(half, shift, i))
    arrived = jnp.concatenate([lab_in[j] for j in range(holders)], axis=0)
    arrived = jnp.concatenate([(arrived // 128).astype(f32), (arrived % 128).astype(f32)], axis=0)
    widen = jnp.where(
        lax.broadcasted_iota(i32, (LANES, total), 1) % pad == lax.broadcasted_iota(i32, (LANES, total), 0),
        1.0, 0.0,
    ).astype(bf16)
    wide = dot(arrived.astype(bf16), widen, ((1,), (0,)))
    wide = wide[:holders] * 128.0 + wide[holders:]
    here = lax.broadcasted_iota(i32, (holders, total), 1) // pad == lax.broadcasted_iota(i32, (holders, total), 0)
    query = jnp.sum(jnp.where(here, wide, 0.0), axis=0, keepdims=True)
    query_first = jnp.floor(query * (1.0 / RANKS)) * RANKS
    key = jnp.transpose(jnp.broadcast_to(query, (LANES, total)))
    for tile in range(total // LANES):
        cut = slice(tile * LANES, (tile + 1) * LANES)
        allowed = (key < query[:, cut]) & (key >= query_first[:, cut])
        bias[:, cut] = jnp.where(allowed, 0.0, -4.0)

    def wait_rows(half, shift, i):
        place = place_of(source_of(half, shift, i), me)
        pltpu.make_async_remote_copy(
            src_ref=outgoing.at[0], dst_ref=incoming.at[place],
            send_sem=row_send.at[me], recv_sem=row_recv.at[place],
            device_id={"hold": me}, device_id_type=MESH,
        ).wait_recv()

    def rows_at(start, end):
        return incoming[start // pad : -(-end // pad)].reshape(-1, features)

    def tile_best(keys, first_key, last_key, queries, tile):
        cut = slice(tile * QUERY_TILE, (tile + 1) * QUERY_TILE)
        scores = dot(keys, queries, ((1,), (1,))) + bias[first_key:last_key, cut]
        return jnp.max(scores, axis=0, keepdims=True)

    early = (GROUPS - 1) * group_rows
    early_tiles = early // QUERY_TILE
    own_rows.wait()
    for half, shift in [(0, 0), (0, 1), (1, 0)]:
        over(half, shift, lambda i: wait_rows(half, shift, i))
    keys = incoming[: (GROUPS - 1) * size].reshape(early, features)
    for tile in range(early_tiles):
        queries = keys[tile * QUERY_TILE : (tile + 1) * QUERY_TILE]
        best[tile] = tile_best(keys, 0, early, queries, tile)
    over(1, 1, lambda i: wait_rows(1, 1, i))
    keys = incoming[...].reshape(total, features)
    for tile in range(total // QUERY_TILE):
        queries = keys[tile * QUERY_TILE : (tile + 1) * QUERY_TILE]
        if tile < early_tiles:
            most = jnp.maximum(best[tile], tile_best(keys[early:], early, total, queries, tile))
        else:
            most = tile_best(keys, 0, total, queries, tile)
        most = jnp.maximum(most, floor_value)
        for k in range(QUERY_TILE // LANES):
            ret[tile * (QUERY_TILE // LANES) + k] = most[:, k * LANES : (k + 1) * LANES]

    def ret_copy(half, shift, i):
        source = source_of(half, shift, i)
        return pltpu.make_async_remote_copy(
            src_ref=ret.at[pl.ds(window_of(place_of(source, me)), 2)], dst_ref=back.at[me],
            send_sem=ret_send.at[source], recv_sem=ret_recv.at[me],
            device_id={"hold": source}, device_id_type=MESH,
        )

    for half, shift in kinds:
        over(half, shift, lambda i: ret_copy(half, shift, i).start())
    own_ret = pltpu.make_async_copy(
        ret.at[pl.ds(window_of(place_of(me, me)), 2)], back.at[me], self_sem.at[2]
    )
    own_ret.start()
    for number, (half, shift) in enumerate(kinds):
        over(half, shift, lambda i: row_copy(number, half, shift, i).wait_send())

    def wait_ret(half, shift, i):
        dest = target_of(half, shift, i)
        pltpu.make_async_remote_copy(
            src_ref=ret.at[pl.ds(0, 2)], dst_ref=back.at[dest],
            send_sem=ret_send.at[me], recv_sem=ret_recv.at[dest],
            device_id={"hold": me}, device_id_type=MESH,
        ).wait_recv()

    own_ret.wait()
    for half, shift in kinds:
        over(half, shift, lambda i: wait_ret(half, shift, i))
    returned = jnp.concatenate(
        [jnp.concatenate([back[j, 0], back[j, 1]], axis=1) for j in range(holders)], axis=0
    )
    picked = dot(pieces_of(returned), pick, ((1,), (0,)))
    picked = picked[:holders] + picked[holders : 2 * holders] + picked[2 * holders :]
    out_ref[...] = jnp.sum(jnp.where(member, picked, 0.0), axis=0, keepdims=True)
    for half, shift in kinds:
        over(half, shift, lambda i: ret_copy(half, shift, i).wait_send())


def shards(embeddings, cluster_id, cluster_rank):
    holders = lax.axis_size("hold")
    rows, features = embeddings.shape
    slot_count = 3 * rows // (2 * holders)
    pad = -(-slot_count // 16) * 16
    total = holders * pad
    vmem = pl.BlockSpec(memory_space=pltpu.VMEM)
    out = pl.pallas_call(
        functools.partial(kernel, holders, pad),
        out_shape=jax.ShapeDtypeStruct((1, rows), f32),
        in_specs=[pl.BlockSpec(memory_space=pl.ANY), vmem, vmem],
        out_specs=vmem,
        scratch_shapes=[
            pltpu.VMEM((rows, features), f32),
            pltpu.VMEM((holders, pad, features), bf16),
            pltpu.VMEM((holders, pad, features), bf16),
            pltpu.VMEM((holders, 1, LANES), i32),
            pltpu.VMEM((holders, 1, LANES), i32),
            pltpu.VMEM((total, total), f32),
            pltpu.VMEM((total // QUERY_TILE, 1, QUERY_TILE), f32),
            pltpu.VMEM((total // LANES, 1, LANES), f32),
            pltpu.VMEM((holders, 2, 1, LANES), f32),
            pltpu.SemaphoreType.DMA,
            pltpu.SemaphoreType.DMA((3,)),
            pltpu.SemaphoreType.DMA((holders,)),
            pltpu.SemaphoreType.DMA((holders,)),
            pltpu.SemaphoreType.DMA((holders,)),
            pltpu.SemaphoreType.DMA((holders,)),
            pltpu.SemaphoreType.DMA((holders,)),
            pltpu.SemaphoreType.DMA((holders,)),
        ],
        compiler_params=pltpu.CompilerParams(
            collective_id=0, has_side_effects=True, vmem_limit_bytes=56 * 1024 * 1024
        ),
    )(embeddings, cluster_id.reshape(1, rows), cluster_rank.reshape(1, rows))
    return out.reshape(rows)


def solution(mesh):
    in_specs = (P(("parts", "hold"), None), P(("parts", "hold")), P(("parts", "hold")))
    out_specs = P(("parts", "hold"))
    return jax.shard_map(shards, mesh=mesh, in_specs=in_specs, out_specs=out_specs, check_vma=False)
```

time: 81.4 us -> 41.4 us (0.51)
  Pallas kernels: 0 us -> 39.9 us
  waiting for transfers between devices: 32.6 us -> 0 us
  starting transfers between devices: 19.6 us -> 0 us
  other arithmetic: 10.1 us -> 0 us
  local copies, waits for them, and re-layouts: 10.3 us -> 1.26 us
  loops' own time: 6.28 us -> 0 us
  matrix products: 1.84 us -> 0 us
    pallas_call x0 -> x1, Pallas kernels: none -> 39.9 us  [shards(): pl.pallas_call(functools.partial(kernel, holders, pad), out_shape=jax.Sha...]
    all_to_all x3 -> x0, waiting for transfers between devices: 32.6 us -> none  [the longest x1 25 us: shards(): lax.all_to_all(outgoing, 'hold', split_axis=0, concat_axis=0, tiled=True)]
    all_to_all x3 -> x0, starting transfers between devices: 19.6 us -> none  [the longest x1 7.49 us: shards(): lax.all_to_all(maxima, 'hold', split_axis=0, concat_axis=0, tiled=True)]
    another operation x1 -> x0, loops' own time: 6.28 us -> none  [dense_best(): lax.map(score_block, block_starts(total_rows, block_rows))]
    scatter x1 -> x0, other arithmetic: 3.64 us -> none  [shards(): jnp.zeros((holders * slot_count, features), jnp.bfloat16).at[target]]
    gather x1 -> x0, local copies, waits for them, and re-layouts: 3.41 us -> none  [shards(): return returned[target]]
    dynamic_slice x9 -> x0, local copies, waits for them, and re-layouts: 2.45 us -> none  [the longest x3 2 us: dense_best(): lax.map(score_block, block_starts(total_rows, block_rows))]
    all_to_all x6 -> x0, local copies, waits for them, and re-layouts: 2.13 us -> none  [the longest x3 1.27 us: shards(): lax.all_to_all(maxima, 'hold', split_axis=0, concat_axis=0, tiled=True)]
  transfers between devices with their start and end apart: 3 -> 0, of which waited for: 3 -> 0; matrix products, arithmetic and copies ran while one was open for 7% -> 0% of each run, Pallas kernels for 0% -> 0%
where the time goes in v1:
time: 41.4 us; the launch traced here: 41.2 us
  Pallas kernels  39.9 us (96%)
  local copies, waits for them, and re-layouts  1.26 us (3%)
    pallas_call x1, Pallas kernels, shards(): pl.pallas_call(functools.partial(kernel, holders, pad), out_shape=jax.Sha...  39.9 us
    unnamed x1, local copies, waits for them, and re-layouts  1.26 us

profile of v1, /device:TPU:0, one launch (start us, length us, event | category | flops | bytes accessed | tf_op | source)
XLA Modules:
  0.0 41.2 jit_solution(8943605913562724642)
XLA Ops:
  0.0 39.9 %shard_map.37 = f32[1,512]{1,0:T(1,128)} custom-call(f32[512,768]{1,0:T(8,128)} %emb_hbm.1, s32[1,512]{1,0:T(1,128)} %bitcast.4, s32[1,512]{1,0:T(1,128)} %bitcast.5), custom_call_target="tpu_custom_call" | custom-call | tf_op jit(solution)/shard_map/pallas_call | solution.py:287
  39.9 1.3 %copy.5 = f32[512]{0:T(512)} copy(f32[512]{0:T(512)} %bitcast.3) | data formatting | bytes 4096

commit v2 on v1

--- a/solution.py
+++ b/solution.py
@@ -48,9 +48,9 @@
 
 def kernel(
     holders, pad,
-    emb_hbm, cid_ref, rank_ref, out_ref,
-    emb, outgoing, incoming, lab_out, lab_in, bias, best, ret, back,
-    emb_sem, self_sem, lab_send, lab_recv, row_send, row_recv, ret_send, ret_recv,
+    emb_hbm, cid_hbm, rank_hbm, out_ref,
+    cid_ref, rank_ref, emb, outgoing, incoming, lab_out, lab_in, bias, best, near, far, back,
+    fetch_sem, self_sem, lab_send, lab_recv, row_send, row_recv, ret_send, ret_recv,
 ):
     size = holders // GROUPS
     rows, features = emb.shape
@@ -59,8 +59,12 @@
     me = lax.axis_index("hold")
     my_group, my_spot = me // size, me % size
 
-    fetch = pltpu.make_async_copy(emb_hbm, emb, emb_sem)
-    fetch.start()
+    fetches = [
+        pltpu.make_async_copy(src, dst, fetch_sem.at[n])
+        for n, (src, dst) in enumerate([(cid_hbm, cid_ref), (rank_hbm, rank_ref), (emb_hbm, emb)])
+    ]
+    for fetch in fetches:
+        fetch.start()
 
     barrier = pltpu.get_barrier_semaphore()
 
@@ -95,9 +99,9 @@
 
         lax.fori_loop(start, end, step, 0, unroll=True if size <= 4 else 1)
 
+    fetches[0].wait()
     cid = cid_ref[...]
     owner = cid // CL_DEV
-    code = (cid - owner * CL_DEV + 1) * RANKS + rank_ref[...]
     ids = lax.broadcasted_iota(i32, (holders, rows), 0)
     member = owner == ids
     member16 = jnp.where(member, 1.0, 0.0).astype(bf16)
@@ -108,19 +112,6 @@
     nth = jnp.sum(jnp.where(member, earlier, 0.0), axis=0, keepdims=True).astype(i32)
     target = owner * pad + nth
 
-    spread = jnp.where(lax.broadcasted_iota(i32, (LANES, rows), 0) == nth, 1.0, 0.0).astype(bf16)
-    high = (code // 128).astype(f32)
-    low = (code % 128).astype(f32)
-    parts = jnp.concatenate(
-        [jnp.where(member, high, 0.0), jnp.where(member, low, 0.0)], axis=0
-    ).astype(bf16)
-    packed = dot(parts, spread, ((1,), (1,)))
-    labels = (packed[:holders] * 128.0 + packed[holders:]).astype(i32)
-    for j in range(holders):
-        lab_out[j] = labels[j : j + 1]
-
-    pl.semaphore_wait(barrier, holders - 1)
-
     def label_copy(half, shift, i):
         dest = target_of(half, shift, i)
         place = place_of(me, dest)
@@ -130,12 +121,26 @@
             device_id={"hold": dest}, device_id_type=MESH,
         )
 
-    for half, shift in kinds:
-        over(half, shift, lambda i: label_copy(half, shift, i).start())
     own_label = pltpu.make_async_copy(lab_out.at[me], lab_in.at[place_of(me, me)], self_sem.at[0])
-    own_label.start()
-
-    fetch.wait()
+
+    def send_labels():
+        fetches[1].wait()
+        code = (cid - owner * CL_DEV + 1) * RANKS + rank_ref[...]
+        spread = jnp.where(lax.broadcasted_iota(i32, (LANES, rows), 0) == nth, 1.0, 0.0).astype(bf16)
+        high = (code // 128).astype(f32)
+        low = (code % 128).astype(f32)
+        parts = jnp.concatenate(
+            [jnp.where(member, high, 0.0), jnp.where(member, low, 0.0)], axis=0
+        ).astype(bf16)
+        packed = dot(parts, spread, ((1,), (1,)))
+        labels = (packed[:holders] * 128.0 + packed[holders:]).astype(i32)
+        for j in range(holders):
+            lab_out[j] = labels[j : j + 1]
+        for kind in kinds:
+            over(*kind, lambda i: label_copy(*kind, i).start())
+        own_label.start()
+
+    fetches[2].wait()
     x = emb[...]
     squares = jnp.sum(x * x, axis=1, keepdims=True)
     normed = (x * lax.rsqrt(squares + epsilon)).astype(bf16)
@@ -155,7 +160,11 @@
         chosen = jnp.where(slot_ids == target - base, 1.0, 0.0).astype(bf16)
         laid = dot(chosen, normed, ((1,), (0,))).astype(bf16)
         outgoing[number * size : (number + 1) * size] = laid.reshape(size, pad, features)
+        if number == 0:
+            pl.semaphore_wait(barrier, holders - 1)
         over(half, shift, lambda i: row_copy(number, half, shift, i).start())
+        if number == HALF - 1:
+            send_labels()
     own_rows = pltpu.make_async_copy(
         outgoing.at[(GROUPS - 1) * size + my_spot], incoming.at[place_of(me, me)], self_sem.at[1]
     )
@@ -210,9 +219,6 @@
             device_id={"hold": me}, device_id_type=MESH,
         ).wait_recv()
 
-    def rows_at(start, end):
-        return incoming[start // pad : -(-end // pad)].reshape(-1, features)
-
     def tile_best(keys, first_key, last_key, queries, tile):
         cut = slice(tile * QUERY_TILE, (tile + 1) * QUERY_TILE)
         scores = dot(keys, queries, ((1,), (1,))) + bias[first_key:last_key, cut]
@@ -229,6 +235,15 @@
         best[tile] = tile_best(keys, 0, early, queries, tile)
     over(1, 1, lambda i: wait_rows(1, 1, i))
     keys = incoming[...].reshape(total, features)
+    def ret_copy(half, shift, i):
+        source = source_of(half, shift, i)
+        bests = near if half == 0 else far
+        return pltpu.make_async_remote_copy(
+            src_ref=bests.at[pl.ds(window_of(place_of(source, me)), 2)], dst_ref=back.at[me],
+            send_sem=ret_send.at[source], recv_sem=ret_recv.at[me],
+            device_id={"hold": source}, device_id_type=MESH,
+        )
+
     for tile in range(total // QUERY_TILE):
         queries = keys[tile * QUERY_TILE : (tile + 1) * QUERY_TILE]
         if tile < early_tiles:
@@ -237,20 +252,18 @@
             most = tile_best(keys, 0, total, queries, tile)
         most = jnp.maximum(most, floor_value)
         for k in range(QUERY_TILE // LANES):
-            ret[tile * (QUERY_TILE // LANES) + k] = most[:, k * LANES : (k + 1) * LANES]
-
-    def ret_copy(half, shift, i):
-        source = source_of(half, shift, i)
-        return pltpu.make_async_remote_copy(
-            src_ref=ret.at[pl.ds(window_of(place_of(source, me)), 2)], dst_ref=back.at[me],
-            send_sem=ret_send.at[source], recv_sem=ret_recv.at[me],
-            device_id={"hold": source}, device_id_type=MESH,
-        )
-
-    for half, shift in kinds:
+            part = most[:, k * LANES : (k + 1) * LANES]
+            number = tile * (QUERY_TILE // LANES) + k
+            far[number] = part
+            if tile < early_tiles:
+                near[number] = part
+        if tile == early_tiles - 1:
+            for half, shift in [(0, 1), (0, 0)]:
+                over(half, shift, lambda i: ret_copy(half, shift, i).start())
+    for half, shift in [(1, 0), (1, 1)]:
         over(half, shift, lambda i: ret_copy(half, shift, i).start())
     own_ret = pltpu.make_async_copy(
-        ret.at[pl.ds(window_of(place_of(me, me)), 2)], back.at[me], self_sem.at[2]
+        near.at[pl.ds(window_of(place_of(me, me)), 2)], back.at[me], self_sem.at[2]
     )
     own_ret.start()
     for number, (half, shift) in enumerate(kinds):
@@ -259,7 +272,7 @@
     def wait_ret(half, shift, i):
         dest = target_of(half, shift, i)
         pltpu.make_async_remote_copy(
-            src_ref=ret.at[pl.ds(0, 2)], dst_ref=back.at[dest],
+            src_ref=far.at[pl.ds(0, 2)], dst_ref=back.at[dest],
             send_sem=ret_send.at[me], recv_sem=ret_recv.at[dest],
             device_id={"hold": me}, device_id_type=MESH,
         ).wait_recv()
@@ -283,13 +296,15 @@
     slot_count = 3 * rows // (2 * holders)
     pad = -(-slot_count // 16) * 16
     total = holders * pad
-    vmem = pl.BlockSpec(memory_space=pltpu.VMEM)
+    early_lanes = (GROUPS - 1) * (total // GROUPS) // QUERY_TILE * QUERY_TILE
     out = pl.pallas_call(
         functools.partial(kernel, holders, pad),
         out_shape=jax.ShapeDtypeStruct((1, rows), f32),
-        in_specs=[pl.BlockSpec(memory_space=pl.ANY), vmem, vmem],
-        out_specs=vmem,
+        in_specs=[pl.BlockSpec(memory_space=pl.ANY)] * 3,
+        out_specs=pl.BlockSpec(memory_space=pltpu.VMEM),
         scratch_shapes=[
+            pltpu.VMEM((1, rows), i32),
+            pltpu.VMEM((1, rows), i32),
             pltpu.VMEM((rows, features), f32),
             pltpu.VMEM((holders, pad, features), bf16),
             pltpu.VMEM((holders, pad, features), bf16),
@@ -297,9 +312,10 @@
             pltpu.VMEM((holders, 1, LANES), i32),
             pltpu.VMEM((total, total), f32),
             pltpu.VMEM((total // QUERY_TILE, 1, QUERY_TILE), f32),
+            pltpu.VMEM((early_lanes // LANES, 1, LANES), f32),
             pltpu.VMEM((total // LANES, 1, LANES), f32),
             pltpu.VMEM((holders, 2, 1, LANES), f32),
-            pltpu.SemaphoreType.DMA,
+            pltpu.SemaphoreType.DMA((3,)),
             pltpu.SemaphoreType.DMA((3,)),
             pltpu.SemaphoreType.DMA((holders,)),
             pltpu.SemaphoreType.DMA((holders,)),

time: 41.4 us -> 43.3 us (1.046)
  Pallas kernels: 39.9 us -> 41.9 us
    pallas_call x1, Pallas kernels: 39.9 us -> 41.9 us  [shards(): pl.pallas_call(functools.partial(kernel, holders, pad), out_shape=jax.Sha...]
where the time goes in v2:
time: 43.3 us; the launch traced here: 43.1 us
  Pallas kernels  41.9 us (97%)
  local copies, waits for them, and re-layouts  1.26 us (3%)
    pallas_call x1, Pallas kernels, shards(): pl.pallas_call(functools.partial(kernel, holders, pad), out_shape=jax.Sha...  41.9 us
    unnamed x1, local copies, waits for them, and re-layouts  1.26 us

profile of v2, /device:TPU:0, one launch (start us, length us, event | category | flops | bytes accessed | tf_op | source)
XLA Modules:
  0.0 43.1 jit_solution(14131832385578354269)
XLA Ops:
  0.0 41.9 %shard_map.37 = f32[1,512]{1,0:T(1,128)} custom-call(f32[512,768]{1,0:T(8,128)} %emb_hbm.1, s32[1,512]{1,0:T(1,128)} %bitcast.4, s32[1,512]{1,0:T(1,128)} %bitcast.5), custom_call_target="tpu_custom_call" | custom-call | tf_op jit(solution)/shard_map/pallas_call | solution.py:300
  41.9 1.3 %copy.5 = f32[512]{0:T(512)} copy(f32[512]{0:T(512)} %bitcast.3) | data formatting | bytes 4096

commit v3 on v2

--- a/solution.py
+++ b/solution.py
@@ -163,7 +163,7 @@
         if number == 0:
             pl.semaphore_wait(barrier, holders - 1)
         over(half, shift, lambda i: row_copy(number, half, shift, i).start())
-        if number == HALF - 1:
+        if number == 0:
             send_labels()
     own_rows = pltpu.make_async_copy(
         outgoing.at[(GROUPS - 1) * size + my_spot], incoming.at[place_of(me, me)], self_sem.at[1]

time: 43.3 us -> 40.3 us (0.931)
  Pallas kernels: 41.9 us -> 38.8 us
    pallas_call x1, Pallas kernels: 41.9 us -> 38.8 us  [shards(): pl.pallas_call(functools.partial(kernel, holders, pad), out_shape=jax.Sha...]
where the time goes in v3:
time: 40.3 us; the launch traced here: 40.1 us
  Pallas kernels  38.8 us (96%)
  local copies, waits for them, and re-layouts  1.26 us (3%)
    pallas_call x1, Pallas kernels, shards(): pl.pallas_call(functools.partial(kernel, holders, pad), out_shape=jax.Sha...  38.8 us
    unnamed x1, local copies, waits for them, and re-layouts  1.26 us

profile of v3, /device:TPU:0, one launch (start us, length us, event | category | flops | bytes accessed | tf_op | source)
XLA Modules:
  0.0 40.1 jit_solution(7342233365006852697)
XLA Ops:
  0.0 38.8 %shard_map.37 = f32[1,512]{1,0:T(1,128)} custom-call(f32[512,768]{1,0:T(8,128)} %emb_hbm.1, s32[1,512]{1,0:T(1,128)} %bitcast.4, s32[1,512]{1,0:T(1,128)} %bitcast.5), custom_call_target="tpu_custom_call" | custom-call | tf_op jit(solution)/shard_map/pallas_call | solution.py:300
  38.8 1.3 %copy.5 = f32[512]{0:T(512)} copy(f32[512]{0:T(512)} %bitcast.3) | data formatting | bytes 4096

commit v4 on v3

--- a/solution.py
+++ b/solution.py
@@ -63,8 +63,6 @@
         pltpu.make_async_copy(src, dst, fetch_sem.at[n])
         for n, (src, dst) in enumerate([(cid_hbm, cid_ref), (rank_hbm, rank_ref), (emb_hbm, emb)])
     ]
-    for fetch in fetches:
-        fetch.start()
 
     barrier = pltpu.get_barrier_semaphore()
 
@@ -75,6 +73,8 @@
         return carry
 
     lax.fori_loop(1, holders, greet, 0)
+    for fetch in fetches:
+        fetch.start()
 
     def place_of(source, target):
         return group_place(source // size, target // size) * size + source % size
@@ -266,8 +266,6 @@
         near.at[pl.ds(window_of(place_of(me, me)), 2)], back.at[me], self_sem.at[2]
     )
     own_ret.start()
-    for number, (half, shift) in enumerate(kinds):
-        over(half, shift, lambda i: row_copy(number, half, shift, i).wait_send())
 
     def wait_ret(half, shift, i):
         dest = target_of(half, shift, i)
@@ -288,6 +286,8 @@
     out_ref[...] = jnp.sum(jnp.where(member, picked, 0.0), axis=0, keepdims=True)
     for half, shift in kinds:
         over(half, shift, lambda i: ret_copy(half, shift, i).wait_send())
+    for number, (half, shift) in enumerate(kinds):
+        over(half, shift, lambda i: row_copy(number, half, shift, i).wait_send())
 
 
 def shards(embeddings, cluster_id, cluster_rank):

time: 40.3 us -> 40.3 us (level)
  no operation moved by 1% of the time
where the time goes in v4:
time: 40.3 us; the launch traced here: 40.1 us
  Pallas kernels  38.9 us (97%)
  local copies, waits for them, and re-layouts  1.26 us (3%)
    pallas_call x1, Pallas kernels, shards(): pl.pallas_call(functools.partial(kernel, holders, pad), out_shape=jax.Sha...  38.9 us
    unnamed x1, local copies, waits for them, and re-layouts  1.26 us

profile of v4, /device:TPU:0, one launch (start us, length us, event | category | flops | bytes accessed | tf_op | source)
XLA Modules:
  0.0 40.1 jit_solution(15658312436039026426)
XLA Ops:
  0.0 38.9 %shard_map.37 = f32[1,512]{1,0:T(1,128)} custom-call(f32[512,768]{1,0:T(8,128)} %emb_hbm.1, s32[1,512]{1,0:T(1,128)} %bitcast.4, s32[1,512]{1,0:T(1,128)} %bitcast.5), custom_call_target="tpu_custom_call" | custom-call | tf_op jit(solution)/shard_map/pallas_call | solution.py:300
  38.9 1.3 %copy.5 = f32[512]{0:T(512)} copy(f32[512]{0:T(512)} %bitcast.3) | data formatting | bytes 4096
